TPU v7x, 512 devices: a whole 4x4x16 slice. The times are simulated.
512 devices in a mesh: rep: 32 (over y, z_hi, core), exp: 16 (over z_lo, x).
Axes of the slice: x: 4, y: 4, z: 16 (z_hi: 4, z_lo: 4; z = z_hi * 4 + z_lo), core: 2. Of those that a mesh axis runs over, the one named last changes fastest.
Arguments:
- tokens: bfloat16 [32, 2048, 1024], P('rep', 'exp'), may hold values from -6 to 6
- cotangent: bfloat16 [32, 2048, 1024], P('rep', 'exp'), may hold values from -4 to 4
- route_ids: int32 [32, 2048, 2], P('rep', 'exp'), may hold values from 0 to 3, all different within a row; in each aligned block of 128 rows (0 to 127, 128 to 255, ..., all dimensions but the last counted through in order) at most 96 rows name the same one
- route_weights: bfloat16 [32, 2048, 2], P('rep', 'exp'), may hold values from 0.19921875 to 1
- gate_weight: bfloat16 [32, 1024, 5632], P('rep', None, 'exp'), may hold values from -0.1875 to 0.1875
- up_weight: bfloat16 [32, 1024, 5632], P('rep', None, 'exp'), may hold values from -0.1875 to 0.1875
- down_weight: bfloat16 [32, 5632, 1024], P('rep', 'exp'), may hold values from -0.15625 to 0.15625
- tracker: bfloat16 [32, 5632, 1024], P('rep', 'exp'), may hold values from -12 to 12
- grad_prev: bfloat16 [32, 5632, 1024], P('rep', 'exp'), may hold values from -12 to 12
- gossip_step: int32 [3], replicated, may hold values from 0 to 2
Outputs:
- token_grad: bfloat16 [32, 2048, 1024], P('rep', 'exp')
- tracker_new: bfloat16 [32, 5632, 1024], P('rep', 'exp')
Inputs may be any that keep to these rules, and one draw needn't show every extreme that they name: `route_ids`: each token names 2 different experts; within each aligned block of 128 tokens of a replica no expert is named by more than 96 tokens, and in some block one expert is named by exactly 96.
All inputs are finite; a program needn't handle non-finite values.
Results may differ from a plain program's by a relative error of at most 0.0058.
Values may be sent and summed in bfloat16 or wider, within the bound.
A program may use at most 64 MiB of HBM per device.

v0:
```python
from functools import partial

import jax
import jax.numpy as jnp
from jax import lax
from jax.sharding import PartitionSpec as P

D = 1024
EXPERTS = 4
TOP = 2
ROUNDS = 3
TOK_DEV = 128
CAP = 96


def from_partner(value, axis, distance):
    mask = 2**distance
    pairs = [(source, source ^ mask) for source in range(lax.axis_size(axis))]
    return lax.ppermute(value, axis, pairs)


def swap_state(state, bit_number):
    return from_partner(state, "rep", bit_number)


def fan_out(buffer, group_size):
    shape = buffer.shape
    spread = jnp.broadcast_to(buffer[:, None], (shape[0], group_size) + shape[1:])
    return spread.reshape((shape[0] * group_size,) + shape[1:])


def shards(
    tokens,
    cotangent,
    route_ids,
    route_weights,
    gate_weight,
    up_weight,
    down_weight,
    tracker,
    grad_prev,
    gossip_step,
):
    exp_count = lax.axis_size("exp")
    group_size = exp_count // EXPERTS
    tok_ids = route_ids[0]
    hits = (tok_ids[:, :, None] == jnp.arange(EXPERTS, dtype=jnp.int32)).astype(jnp.int32)
    flat_hits = hits.reshape(-1, EXPERTS)
    slot_rank = jnp.cumsum(flat_hits, axis=0) - 1
    within = jnp.sum(flat_hits * slot_rank, axis=-1).reshape(tok_ids.shape)
    slot_pos = tok_ids * CAP + within
    placed = (slot_pos[:, :, None] == jnp.arange(EXPERTS * CAP, dtype=jnp.int32)).astype(
        jnp.bfloat16
    )
    spread = jnp.sum(placed, axis=1)
    sent_in = jnp.einsum("tc,td->cd", spread, tokens[0], preferred_element_type=jnp.float32).astype(
        jnp.bfloat16
    )
    sent_cot = jnp.einsum(
        "tc,td->cd", spread, cotangent[0], preferred_element_type=jnp.float32
    ).astype(jnp.bfloat16)
    sent_coef = jnp.einsum(
        "tkc,tk->c", placed, route_weights[0], preferred_element_type=jnp.float32
    ).astype(jnp.bfloat16)
    sent_in = fan_out(sent_in.reshape(EXPERTS, CAP, D), group_size)
    sent_cot = fan_out(sent_cot.reshape(EXPERTS, CAP, D), group_size)
    sent_coef = fan_out(sent_coef.reshape(EXPERTS, CAP), group_size)
    w_gate = gate_weight[0]
    w_up = up_weight[0]
    w_down = down_weight[0]
    rows_total = exp_count * CAP
    got_in, got_cot, got_coef = (
        lax.all_to_all(sent_in, "exp", split_axis=0, concat_axis=0, tiled=True),
        lax.all_to_all(sent_cot, "exp", split_axis=0, concat_axis=0, tiled=True),
        lax.all_to_all(sent_coef, "exp", split_axis=0, concat_axis=0, tiled=True),
    )
    x_rows = got_in.reshape(rows_total, D)
    gate_act = jnp.dot(x_rows, w_gate, preferred_element_type=jnp.float32)
    up_act = jnp.dot(x_rows, w_up, preferred_element_type=jnp.float32)
    cot_rows = got_cot.reshape(rows_total, D)
    coef = got_coef.reshape(rows_total, 1).astype(jnp.float32)
    sigmoid_g = jax.nn.sigmoid(gate_act)
    act = gate_act * sigmoid_g
    weighted = (coef * act * up_act).astype(jnp.bfloat16)
    grad = jnp.einsum("rh,rd->hd", weighted, cot_rows, preferred_element_type=jnp.float32)
    hidden_grad = coef * jnp.einsum(
        "rd,hd->rh", cot_rows, w_down, preferred_element_type=jnp.float32
    )
    gate_grad = (hidden_grad * up_act * sigmoid_g * (1.0 + gate_act * (1.0 - sigmoid_g))).astype(
        jnp.bfloat16
    )
    up_grad = (hidden_grad * act).astype(jnp.bfloat16)
    partial_rows = jnp.einsum("rh,dh->rd", gate_grad, w_gate, preferred_element_type=jnp.float32)
    partial_rows = partial_rows + jnp.einsum(
        "rh,dh->rd", up_grad, w_up, preferred_element_type=jnp.float32
    )
    partial_rows = partial_rows.astype(jnp.bfloat16).reshape(exp_count, CAP, D)
    came_back = lax.all_to_all(partial_rows, "exp", split_axis=0, concat_axis=0, tiled=True)
    summed = jnp.sum(came_back.reshape(EXPERTS, group_size, CAP, D).astype(jnp.float32), axis=1)
    summed = summed.reshape(EXPERTS * CAP, D)
    picked = summed[slot_pos.reshape(-1)].reshape(TOK_DEV, TOP, D)
    token_grad = jnp.sum(picked, axis=1).astype(jnp.bfloat16)[None]
    branches = [partial(swap_state, bit_number=bit) for bit in range(3)]
    delta_share = (grad - grad_prev[0].astype(jnp.float32)) / ROUNDS
    mixed = tracker[0].astype(jnp.float32)
    for round_index in range(ROUNDS):
        peer_state = lax.switch(jnp.clip(gossip_step[round_index], 0, 2), branches, mixed)
        mixed = (mixed + peer_state) * 0.5 + delta_share
    return (token_grad, mixed.astype(jnp.bfloat16)[None])


def solution(mesh):
    in_specs = (
        P("rep", "exp", None),
        P("rep", "exp", None),
        P("rep", "exp", None),
        P("rep", "exp", None),
        P("rep", None, "exp"),
        P("rep", None, "exp"),
        P("rep", "exp", None),
        P("rep", "exp", None),
        P("rep", "exp", None),
        P(),
    )
    out_specs = (P("rep", "exp", None), P("rep", "exp", None))
    return jax.shard_map(shards, mesh=mesh, in_specs=in_specs, out_specs=out_specs, check_vma=False)
```

profile of v0, /device:TPU:153, one launch (start us, length us, event | category | flops | bytes accessed | tf_op | source)
XLA Modules:
  0.0 400.5 jit_solution(17162906078777180521)
XLA Ops:
  1.8 1.2 reduce-window.6
  5.3 8.2 %all-to-all-start = ((bf16[16,1,96]{2,1,0:T(2,128)(2,1)}), bf16[16,1,96]{2,1,0:T(2,128)(2,1)S(1)}, u32[]{:S(2)}, u32[]{:S(2)}) async-start(bf16[16,1,96]{2,1,0:T(2,128)(2,1)} %copy.37), calls=%async_computation | async-start | bytes 16384 | tf_op jit(solution)/shard_map/all_to_all | solution.py:75
  13.6 1.3 convolution_convert_fusion
  14.9 5.2 %all-to-all-done = bf16[16,1,96]{2,1,0:T(2,128)(2,1)S(1)} async-done(((bf16[16,1,96]{2,1,0:T(2,128)(2,1)}), bf16[16,1,96]{2,1,0:T(2,128)(2,1)S(1)}, u32[]{:S(2)}, u32[]{:S(2)}) %all-to-all-start) | async-done | bytes 3104 | tf_op jit(solution)/shard_map/all_to_all | solution.py:75
  20.2 2.1 broadcast_in_dim.34
  22.3 4.6 %all-to-all-start.2 = ((bf16[16,96,1024]{2,1,0:T(8,128)(2,1)}), bf16[16,96,1024]{2,1,0:T(8,128)(2,1)}, u32[]{:S(2)}, u32[]{:S(2)}) async-start(bf16[16,96,1024]{2,1,0:T(8,128)(2,1)} %bitcast.76), calls=%async_computation.2 | async-start | bytes 6291456 | tf_op jit(solution)/shard_map/all_to_all | solution.py:73
  27.3 59.3 %all-to-all-done.2 = bf16[16,96,1024]{2,1,0:T(8,128)(2,1)} async-done(((bf16[16,96,1024]{2,1,0:T(8,128)(2,1)}), bf16[16,96,1024]{2,1,0:T(8,128)(2,1)}, u32[]{:S(2)}, u32[]{:S(2)}) %all-to-all-start.2) | async-done | bytes 3145760 | tf_op jit(solution)/shard_map/all_to_all | solution.py:73
  86.6 2.1 broadcast_in_dim.32
  88.7 15.4 %all-to-all-start.1 = ((bf16[16,96,1024]{2,1,0:T(8,128)(2,1)}), bf16[16,96,1024]{2,1,0:T(8,128)(2,1)}, u32[]{:S(2)}, u32[]{:S(2)}) async-start(bf16[16,96,1024]{2,1,0:T(8,128)(2,1)} %bitcast.75), calls=%async_computation.1 | async-start | bytes 6291456 | tf_op jit(solution)/shard_map/all_to_all | solution.py:74
  104.2 4.6 %fusion.7 = f32[1536,352]{0,1:T(8,128)} fusion(bf16[1536,1024]{1,0:T(8,128)(2,1)} %bitcast.14, bf16[1,1024,352]{1,2,0:T(8,128)(2,1)S(1)} %copy-done), kind=kOutput, calls=%fused_computation.23 | convolution fusion | flops 1107296256 | bytes 6029312 | tf_op jit(solution)/shard_map/dot_general | solution.py:78
  108.8 4.7 %fusion.10 = f32[1536,352]{0,1:T(8,128)} fusion(bf16[1536,1024]{1,0:T(8,128)(2,1)} %bitcast.14, bf16[1,1024,352]{1,2,0:T(8,128)(2,1)S(1)} %copy-done.7), kind=kOutput, calls=%fused_computation.26 | convolution fusion | flops 1107296256 | bytes 6029312 | tf_op jit(solution)/shard_map/dot_general | solution.py:79
  113.6 50.4 %all-to-all-done.1 = bf16[16,96,1024]{2,1,0:T(8,128)(2,1)} async-done(((bf16[16,96,1024]{2,1,0:T(8,128)(2,1)}), bf16[16,96,1024]{2,1,0:T(8,128)(2,1)}, u32[]{:S(2)}, u32[]{:S(2)}) %all-to-all-start.1) | async-done | bytes 3145760 | tf_op jit(solution)/shard_map/all_to_all | solution.py:74
  164.0 3.4 convolution_multiply_fusion
  167.4 2.4 fusion.2
  169.7 3.8 add_convert_fusion
  173.5 15.5 %all-to-all-start.3 = ((bf16[16,96,1024]{2,1,0:T(8,128)(2,1)}), bf16[16,96,1024]{2,1,0:T(8,128)(2,1)}, u32[]{:S(2)}, u32[]{:S(2)}) async-start(bf16[16,96,1024]{2,1,0:T(8,128)(2,1)} %bitcast.77), calls=%async_computation.3 | async-start | bytes 6291456 | tf_op jit(solution)/shard_map/all_to_all | solution.py:98
  191.8 176.9 %conditional.3 = (f32[352,1024]{1,0:T(8,128)}) conditional(s32[]{:T(128)} %bitcast.24, f32[352,1024]{1,0:T(8,128)S(1)} %bitcast_convert_fusion, f32[352,1024]{1,0:T(8,128)S(1)} %bitcast_convert_fusion, f32[352,1024]{1,0:T(8,128)S(1)} %bitcast_convert_fusion), branch_computations={%region_6.7_spmd, %region_7.8_spmd, %region_8.9_spmd} | conditional | bytes 5767216 | solution.py:107
  191.8 7.9 %collective-permute-start.2 = (f32[352,1024]{1,0:T(8,128)S(1)}, f32[352,1024]{1,0:T(8,128)}, u32[]{:S(2)}, u32[]{:S(2)}) collective-permute-start(f32[352,1024]{1,0:T(8,128)S(1)} %param.2), channel_id=1, source_target_pairs={{0,64},{16,80},{32,96},{48,112},{64,0},{80,16},{96,32},{112,48},{1... | collective-permute-start | bytes 4325384 | tf_op jit(solution)/shard_map/cond/branch_2_fun/ppermute | solution.py:19
  199.7 168.9 %collective-permute-done.2 = f32[352,1024]{1,0:T(8,128)} collective-permute-done((f32[352,1024]{1,0:T(8,128)S(1)}, f32[352,1024]{1,0:T(8,128)}, u32[]{:S(2)}, u32[]{:S(2)}) %collective-permute-start.2) | collective-permute-done | bytes 1441824 | tf_op jit(solution)/shard_map/cond/branch_2_fun/ppermute | solution.py:19
  368.7 5.2 %multiply_add_fusion.1 = (f32[352,1024]{1,0:T(8,128)S(1)}, f32[352,1024]{1,0:T(8,128)S(1)}) fusion(f32[352,1024]{1,0:T(8,128)} %get-tuple-element.28, bf16[1,352,1024]{2,1,0:T(8,128)(2,1)S(1)} %copy-done.3, bf16[1,352,1024]{2,1,0:T(8,128)(2,1)} %param.27, bf16[1536,1024]{1,0:T(8,128)(2,1)} %bitcast.9, f32[1536,352]{0,1:T(8,128)} %fusion.10, ...), kind=kOutput, calls=%fused_computation.13 | convolution fusion | flops 1113604096 | bytes 13244416 | tf_op jit(solution)/shard_map/rh,rd->hd/dot_general | solution.py:85
  373.9 1.1 copy-done.2
  375.0 7.3 %conditional.4 = (f32[352,1024]{1,0:T(8,128)}) conditional(s32[]{:T(128)} %bitcast.27, f32[352,1024]{1,0:T(8,128)S(1)} %get-tuple-element.26, f32[352,1024]{1,0:T(8,128)S(1)} %get-tuple-element.26, f32[352,1024]{1,0:T(8,128)S(1)} %get-tuple-element.26), branch_computations={%region_9.10_spmd, %region_10.11_spmd, %region_11.12_spmd} | conditional | bytes 5767216 | solution.py:107
  375.0 4.4 %collective-permute-start.3 = (f32[352,1024]{1,0:T(8,128)S(1)}, f32[352,1024]{1,0:T(8,128)}, u32[]{:S(2)}, u32[]{:S(2)}) collective-permute-start(f32[352,1024]{1,0:T(8,128)S(1)} %param.3), channel_id=1, source_target_pairs={{0,16},{16,0},{32,48},{48,32},{64,80},{80,64},{96,112},{112,96},{1... | collective-permute-start | bytes 4325384 | tf_op jit(solution)/shard_map/cond/branch_0_fun/ppermute | solution.py:19
  379.4 3.0 collective-permute-done.3
  382.4 2.2 multiply_add_fusion
  384.6 1.1 copy-done.1
  385.7 5.2 %conditional.5 = (f32[352,1024]{1,0:T(8,128)}) conditional(s32[]{:T(128)} %bitcast.28, f32[352,1024]{1,0:T(8,128)S(1)} %multiply_add_fusion, f32[352,1024]{1,0:T(8,128)S(1)} %multiply_add_fusion, f32[352,1024]{1,0:T(8,128)S(1)} %multiply_add_fusion), branch_computations={%region_12.13_spmd, %region_13.14_spmd, %region_14.15_spmd} | conditional | bytes 5767216 | solution.py:107
  385.7 2.3 collective-permute-start.6
  388.0 3.0 collective-permute-done.6
  390.9 3.1 fusion.5
  394.1 2.7 convert_reduce_fusion
  398.5 2.1 reduce_sum.45
  (49 shorter events, 6.6 us)
Async XLA Ops:
  0.6 103.6 %copy-start = (bf16[1,1024,352]{1,2,0:T(8,128)(2,1)S(1)}, bf16[1,1024,352]{1,2,0:T(8,128)(2,1)}, u32[]{:S(2)}) copy-start(bf16[1,1024,352]{1,2,0:T(8,128)(2,1)} %param.23) | copy-start | bytes 2162692
  5.3 14.9 %all-to-all-start = ((bf16[16,1,96]{2,1,0:T(2,128)(2,1)}), bf16[16,1,96]{2,1,0:T(2,128)(2,1)S(1)}, u32[]{:S(2)}, u32[]{:S(2)}) async-start(bf16[16,1,96]{2,1,0:T(2,128)(2,1)} %copy.37), calls=%async_computation | async-start | bytes 16384 | tf_op jit(solution)/shard_map/all_to_all | solution.py:75
  22.3 4.6 %copy-start.4 = (bf16[1,128,1024]{2,1,0:T(8,128)(2,1)S(1)}, bf16[1,128,1024]{2,1,0:T(8,128)(2,1)}, u32[]{:S(2)}) copy-start(bf16[1,128,1024]{2,1,0:T(8,128)(2,1)} %param.20) | copy-start | bytes 786436
  22.3 64.3 %all-to-all-start.2 = ((bf16[16,96,1024]{2,1,0:T(8,128)(2,1)}), bf16[16,96,1024]{2,1,0:T(8,128)(2,1)}, u32[]{:S(2)}, u32[]{:S(2)}) async-start(bf16[16,96,1024]{2,1,0:T(8,128)(2,1)} %bitcast.76), calls=%async_computation.2 | async-start | bytes 6291456 | tf_op jit(solution)/shard_map/all_to_all | solution.py:73
  88.7 75.2 %all-to-all-start.1 = ((bf16[16,96,1024]{2,1,0:T(8,128)(2,1)}), bf16[16,96,1024]{2,1,0:T(8,128)(2,1)}, u32[]{:S(2)}, u32[]{:S(2)}) async-start(bf16[16,96,1024]{2,1,0:T(8,128)(2,1)} %bitcast.75), calls=%async_computation.1 | async-start | bytes 6291456 | tf_op jit(solution)/shard_map/all_to_all | solution.py:74
  104.2 4.6 %copy-start.7 = (bf16[1,1024,352]{1,2,0:T(8,128)(2,1)S(1)}, bf16[1,1024,352]{1,2,0:T(8,128)(2,1)}, u32[]{:S(2)}) copy-start(bf16[1,1024,352]{1,2,0:T(8,128)(2,1)} %param.24) | copy-start | bytes 2162692
  108.8 55.1 %copy-start.6 = (bf16[1,352,1024]{2,1,0:T(8,128)(2,1)S(1)}, bf16[1,352,1024]{2,1,0:T(8,128)(2,1)}, u32[]{:S(2)}) copy-start(bf16[1,352,1024]{2,1,0:T(8,128)(2,1)} %param.25) | copy-start | bytes 2162692
  164.0 3.4 copy-start.8
  164.0 3.4 copy-start.9
  173.5 15.5 %copy-start.5 = (s32[3]{0:T(128)S(1)}, s32[3]{0:T(128)}, u32[]{:S(2)}) copy-start(s32[3]{0:T(128)} %param.28) | copy-start | bytes 40
  173.5 18.1 %copy-start.3 = (bf16[1,352,1024]{2,1,0:T(8,128)(2,1)S(1)}, bf16[1,352,1024]{2,1,0:T(8,128)(2,1)}, u32[]{:S(2)}) copy-start(bf16[1,352,1024]{2,1,0:T(8,128)(2,1)} %param.26) | copy-start | bytes 2162692
  173.5 220.6 %all-to-all-start.3 = ((bf16[16,96,1024]{2,1,0:T(8,128)(2,1)}), bf16[16,96,1024]{2,1,0:T(8,128)(2,1)}, u32[]{:S(2)}, u32[]{:S(2)}) async-start(bf16[16,96,1024]{2,1,0:T(8,128)(2,1)} %bitcast.77), calls=%async_computation.3 | async-start | bytes 6291456 | tf_op jit(solution)/shard_map/all_to_all | solution.py:98
  191.8 176.9 %collective-permute-start.2 = (f32[352,1024]{1,0:T(8,128)S(1)}, f32[352,1024]{1,0:T(8,128)}, u32[]{:S(2)}, u32[]{:S(2)}) collective-permute-start(f32[352,1024]{1,0:T(8,128)S(1)} %param.2), channel_id=1, source_target_pairs={{0,64},{16,80},{32,96},{48,112},{64,0},{80,16},{96,32},{112,48},{1... | collective-permute-start | bytes 4325384 | tf_op jit(solution)/shard_map/cond/branch_2_fun/ppermute | solution.py:19
  373.9 1.1 copy-start.2
  375.0 7.3 %collective-permute-start.3 = (f32[352,1024]{1,0:T(8,128)S(1)}, f32[352,1024]{1,0:T(8,128)}, u32[]{:S(2)}, u32[]{:S(2)}) collective-permute-start(f32[352,1024]{1,0:T(8,128)S(1)} %param.3), channel_id=1, source_target_pairs={{0,16},{16,0},{32,48},{48,32},{64,80},{80,64},{96,112},{112,96},{1... | collective-permute-start | bytes 4325384 | tf_op jit(solution)/shard_map/cond/branch_0_fun/ppermute | solution.py:19
  384.6 1.1 copy-start.1
  385.7 5.2 %collective-permute-start.6 = (f32[352,1024]{1,0:T(8,128)S(1)}, f32[352,1024]{1,0:T(8,128)}, u32[]{:S(2)}, u32[]{:S(2)}) collective-permute-start(f32[352,1024]{1,0:T(8,128)S(1)} %param.6), channel_id=1, source_target_pairs={{0,16},{16,0},{32,48},{48,32},{64,80},{80,64},{96,112},{112,96},{1... | collective-permute-start | bytes 4325384 | tf_op jit(solution)/shard_map/cond/branch_0_fun/ppermute | solution.py:19
where the time goes:
time: 401 us
  waiting for transfers between devices  290 us (72%)
  starting transfers between devices  58.2 us (15%)
  matrix products  26.7 us (7%)
  other arithmetic  11.8 us (3%)
  local copies, waits for them, and re-layouts  11.2 us (3%)
    ppermute x3, waiting for transfers between devices, from_partner(): return lax.ppermute(value, axis, pairs)  175 us
    all_to_all x1, waiting for transfers between devices, shards(): lax.all_to_all(sent_in, 'exp', split_axis=0, concat_axis=0, tiled=True)  59.3 us
    all_to_all x1, waiting for transfers between devices, shards(): lax.all_to_all(sent_cot, 'exp', split_axis=0, concat_axis=0, tiled=True)  50.4 us
    all_to_all x1, starting transfers between devices, shards(): lax.all_to_all(partial_rows, 'exp', split_axis=0, concat_axis=0, tiled=True)  15.5 us
    all_to_all x1, starting transfers between devices, shards(): lax.all_to_all(sent_cot, 'exp', split_axis=0, concat_axis=0, tiled=True)  15.4 us
    ppermute x3, starting transfers between devices, from_partner(): return lax.ppermute(value, axis, pairs)  14.6 us
    all_to_all x1, starting transfers between devices, shards(): lax.all_to_all(sent_coef, 'exp', split_axis=0, concat_axis=0, tiled=True)  8.19 us
  transfers between devices with their start and end apart: 7, of which 6 were waited for; matrix products, arithmetic and copies ran while one was open for 6% of the time, Pallas kernels for 0%

commit v1 on v0

v1 whole, which is shorter than its diff:
```python
from functools import partial

import jax
import jax.numpy as jnp
from jax import lax
from jax.experimental import pallas as pl
from jax.experimental.pallas import tpu as pltpu
from jax.sharding import PartitionSpec as P

D = 1024
EXPERTS = 4
ROUNDS = 3
TOK = 128
CAP = 96
HID = 352
COLS = 4 * CAP
ORDER = (1, 3, 2)
F32 = jnp.float32
BF16 = jnp.bfloat16
NT = (((1,), (1,)), ((), ()))
TN = (((0,), (0,)), ((), ()))
NN = (((1,), (0,)), ((), ()))


def dot(a, b, dims=NN):
    return lax.dot_general(a, b, dims, preferred_element_type=F32)


def layer_kernel(
    tok_ref,
    cot_ref,
    ids_ref,
    wts_ref,
    gate_ref,
    up_ref,
    down_ref,
    out_ref,
    grad_ref,
    stage,
    spread,
    rows,
    weights,
    gu,
    hd,
    gug,
    wtd,
    part,
    grads,
    gsend,
    grecv,
    psend,
    precv,
    ret,
    zsend,
    z_ss,
    z_rs,
    a_ss,
    a_rs,
    w_ss,
    w_rs,
    g_ss,
    g_rs,
    p_ss,
    p_rs,
    r_ss,
    r_rs,
):
    rep = lax.axis_index("rep")
    e = lax.axis_index("exp")
    z = e // 4
    x = e - 4 * z
    odd = x % 2
    pair = e + 1 - 2 * odd
    mate = 4 * z + (x + 3 + 2 * odd) % 4

    def at_z(d):
        return 4 * ((z + d) % 4) + x

    def send(src, dst, ss, rs, to):
        return pltpu.make_async_remote_copy(
            src_ref=src,
            dst_ref=dst,
            send_sem=ss,
            recv_sem=rs,
            device_id=(rep, to),
            device_id_type=pl.DeviceIdType.MESH,
        )

    barrier = pltpu.get_barrier_semaphore()
    for peer in (at_z(1), at_z(2), at_z(3), pair, mate):
        pl.semaphore_signal(
            barrier, inc=1, device_id=(rep, peer), device_id_type=pl.DeviceIdType.MESH
        )

    weights[0, 0:HID] = gate_ref[...].T
    pl.semaphore_wait(barrier, 5)

    def w_copy(i):
        piece = pl.ds(i * HID, HID)
        return send(weights.at[0, piece], weights.at[1, piece], w_ss.at[i], w_rs.at[i], mate)

    w_copy(0).start()

    lane = lax.broadcasted_iota(jnp.int32, (TOK, TOK), 1)
    sub = lax.broadcasted_iota(jnp.int32, (TOK, TOK), 0)
    id0 = ids_ref[:, 0:1]
    id1 = ids_ref[:, 1:2]
    hit0 = (lane == id0).astype(F32)
    hit1 = (lane == id1).astype(F32)
    wts = wts_ref[...].astype(F32)
    hits = (hit0 + hit1).astype(BF16)
    coefs = (hit0 * wts[:, 0:1] + hit1 * wts[:, 1:2]).astype(BF16)
    eye = (sub == lane).astype(F32).astype(BF16)
    before = (sub < lane).astype(F32).astype(BF16)
    hit_t = dot(hits, eye, TN)[0:8]
    rank_t = dot(hits, before, TN)[0:8]
    coef_t = dot(coefs, eye, TN)[0:8]
    expert = lax.broadcasted_iota(jnp.int32, (8, TOK), 0)
    slot = lax.broadcasted_iota(jnp.int32, (CAP, TOK), 0).astype(F32)

    def place(d):
        mine = expert == (z + d) % 4
        zero = jnp.zeros((8, TOK), F32)
        hit = jnp.sum(jnp.where(mine, hit_t, zero), axis=0, keepdims=True)
        rank = jnp.sum(jnp.where(mine, rank_t, zero), axis=0, keepdims=True)
        coef = jnp.sum(jnp.where(mine, coef_t, zero), axis=0, keepdims=True)
        placed = jnp.where(slot == rank, 1.0, 0.0) * hit
        plain = placed.astype(BF16)
        spread[d * CAP:(d + 1) * CAP] = plain
        t = dot(plain, tok_ref[...]).astype(BF16)
        c = dot((placed * coef).astype(BF16), cot_ref[...]).astype(BF16)
        return t, c

    def z_copy(d):
        return send(stage.at[d], rows.at[0, :, z], z_ss.at[d], z_rs.at[d], at_z(d))

    def z_arrive(d):
        return send(stage.at[d], rows.at[0, :, (z + 4 - d) % 4], z_ss.at[d], z_rs.at[d], at_z(d))

    def a_copy(d):
        zs = (z + 4 - d) % 4
        return send(rows.at[0, :, zs], rows.at[1, :, zs], a_ss.at[d], a_rs.at[d], pair)

    for d in (2, 1, 3):
        t, c = place(d)
        stage[d, 0] = t
        stage[d, 1] = c
        z_copy(d).start()
    t, c = place(0)
    rows[0, 0, z] = t
    rows[0, 1, z] = c
    a_copy(0).start()

    weights[0, HID:2 * HID] = up_ref[...].T
    w_copy(1).start()
    weights[0, 2 * HID:3 * HID] = down_ref[...]

    for d in ORDER:
        if d == 2:
            w_copy(0).wait_send()
            w_copy(1).wait_send()
            w_copy(2).start()
        z_arrive(d).wait_recv()
        a_copy(d).start()

    def first(rg, hs):
        tk = rows[rg, 0].reshape(COLS, D)
        unit = 2 * rg + hs
        gu[unit] = dot(weights[hs, 0:2 * HID], tk, NT)

        def body(i, carry):
            at = pl.ds(pl.multiple_of(i * 32, 32), 32)
            low = pl.ds(pl.multiple_of(i * 32 + HID, 32), 32)
            g = gu[unit, at]
            u = gu[unit, low]
            wtd[at] = (g * jax.nn.sigmoid(g) * u).astype(BF16)
            return carry

        lax.fori_loop(0, HID // 32, body, 0)
        return dot(wtd[...], rows[rg, 1].reshape(COLS, D))

    def second(rg, hs):
        unit = 2 * rg + hs
        hd[...] = dot(weights[hs, 2 * HID:3 * HID], rows[rg, 1].reshape(COLS, D), NT)

        def body(i, carry):
            at = pl.ds(pl.multiple_of(i * 32, 32), 32)
            low = pl.ds(pl.multiple_of(i * 32 + HID, 32), 32)
            g = gu[unit, at]
            u = gu[unit, low]
            h = hd[at]
            s = jax.nn.sigmoid(g)
            gug[at] = (h * u * s * (1.0 + g * (1.0 - s))).astype(BF16)
            gug[low] = (h * (g * s)).astype(BF16)
            return carry

        lax.fori_loop(0, HID // 32, body, 0)
        return dot(gug[...], weights[hs, 0:2 * HID], TN)

    grads[...] = first(0, 0)
    part[0] = second(0, 0).reshape(4, CAP, D)

    w_copy(0).wait_recv()
    w_copy(1).wait_recv()
    other = first(0, 1)
    for d in range(4):
        a_copy(d).wait_recv()
    gsend[...] = (other + first(1, 1)).astype(BF16)
    g_copy = send(gsend, grecv, g_ss, g_rs, mate)
    g_copy.start()
    grads[...] += first(1, 0)

    w_copy(2).wait_recv()
    part[1] = second(1, 0).reshape(4, CAP, D)
    psend[...] = (part[1] + second(1, 1).reshape(4, CAP, D)).astype(BF16)

    def p_copy(d):
        zs = (z + d) % 4
        return send(psend.at[zs], precv.at[zs], p_ss.at[d], p_rs.at[d], pair)

    for d in (2, 1, 3, 0):
        p_copy(d).start()
    part[0] += second(0, 1).reshape(4, CAP, D)

    def r_copy(d):
        return send(zsend.at[d], ret.at[4 - d], r_ss.at[d], r_rs.at[4 - d], at_z(d))

    for d in (2, 1, 3, 0):
        p_copy(d).wait_recv()
        zs = (z + d) % 4
        total = (part[0, zs] + precv[zs].astype(F32)).astype(BF16)
        if d == 0:
            ret[0] = total
        else:
            zsend[d] = total
            r_copy(d).start()

    g_copy.wait_recv()
    grad_ref[...] = grads[...] + grecv[...].astype(F32)

    for d in (1, 3, 2):
        r_copy(d).wait_recv()
    out_ref[...] = dot(spread[...], ret[...].reshape(COLS, D), TN).astype(BF16)

    for d in (1, 2, 3):
        z_copy(d).wait_send()
        r_copy(d).wait_send()
    for d in range(4):
        a_copy(d).wait_send()
        p_copy(d).wait_send()
    w_copy(2).wait_send()
    g_copy.wait_send()


def layer(tokens, cotangent, route_ids, route_weights, gate, up, down):
    vmem = pl.BlockSpec(memory_space=pltpu.VMEM)
    dma = pltpu.SemaphoreType.DMA
    return pl.pallas_call(
        layer_kernel,
        out_shape=(
            jax.ShapeDtypeStruct((TOK, D), BF16),
            jax.ShapeDtypeStruct((HID, D), F32),
        ),
        in_specs=[vmem] * 7,
        out_specs=(vmem, vmem),
        scratch_shapes=[
            pltpu.VMEM((4, 2, CAP, D), BF16),
            pltpu.VMEM((COLS, TOK), BF16),
            pltpu.VMEM((2, 2, 4, CAP, D), BF16),
            pltpu.VMEM((2, 3 * HID, D), BF16),
            pltpu.VMEM((4, 2 * HID, COLS), F32),
            pltpu.VMEM((HID, COLS), F32),
            pltpu.VMEM((2 * HID, COLS), BF16),
            pltpu.VMEM((HID, COLS), BF16),
            pltpu.VMEM((2, 4, CAP, D), F32),
            pltpu.VMEM((HID, D), F32),
            pltpu.VMEM((HID, D), BF16),
            pltpu.VMEM((HID, D), BF16),
            pltpu.VMEM((4, CAP, D), BF16),
            pltpu.VMEM((4, CAP, D), BF16),
            pltpu.VMEM((4, CAP, D), BF16),
            pltpu.VMEM((4, CAP, D), BF16),
            dma((4,)),
            dma((4,)),
            dma((4,)),
            dma((4,)),
            dma((3,)),
            dma((3,)),
            dma,
            dma,
            dma((4,)),
            dma((4,)),
            dma((4,)),
            dma((4,)),
        ],
        compiler_params=pltpu.CompilerParams(
            collective_id=0, has_side_effects=True, vmem_limit_bytes=56 * 2**20
        ),
        cost_estimate=pl.CostEstimate(
            flops=7 * 10**9, bytes_accessed=6 * 10**6, transcendentals=10**6
        ),
    )(tokens, cotangent, route_ids, route_weights, gate, up, down)


def average(state, bit):
    count = lax.axis_size("rep")
    pairs = [(source, source ^ (1 << bit)) for source in range(count)]
    peer = lax.ppermute(state.astype(BF16), "rep", pairs)
    return (state + peer.astype(F32)) * 0.5


def shards(
    tokens,
    cotangent,
    route_ids,
    route_weights,
    gate_weight,
    up_weight,
    down_weight,
    tracker,
    grad_prev,
    gossip_step,
):
    out, grad = layer(
        tokens[0],
        cotangent[0],
        route_ids[0],
        route_weights[0],
        gate_weight[0],
        up_weight[0],
        down_weight[0],
    )
    steps = jnp.clip(gossip_step, 0, 2)
    s1, s2, s3 = steps[0], steps[1], steps[2]
    averages = [partial(average, bit=bit) for bit in range(3)]
    maybe = [lambda state: state] + averages
    mixed = tracker[0].astype(F32)
    mixed = lax.switch(jnp.where((s1 == s2) | (s1 == s3), 0, s1 + 1), maybe, mixed)
    share = (grad - grad_prev[0].astype(F32)) / ROUNDS
    mixed = lax.switch(jnp.where(s2 == s3, 0, s2 + 1), maybe, mixed + share)
    mixed = lax.switch(s3, averages, mixed + share) + share
    return (out[None], mixed.astype(BF16)[None])


def solution(mesh):
    rows = P("rep", "exp", None)
    cols = P("rep", None, "exp")
    in_specs = (rows, rows, rows, rows, cols, cols, rows, rows, rows, P())
    return jax.shard_map(
        shards, mesh=mesh, in_specs=in_specs, out_specs=(rows, rows), check_vma=False
    )
```

time: 401 us -> 201 us (0.50)
  the two profiles are of different devices: /device:TPU:153 before, /device:TPU:40 now
where the time goes in v1:
time: 201 us
  Pallas kernels  96.4 us (48%)
  waiting for transfers between devices  62.1 us (31%)
  starting transfers between devices  16.9 us (8%)
  local copies, waits for them, and re-layouts  10.3 us (5%)
  other arithmetic  8.36 us (4%)
  between operations  6.45 us (3%)
    pallas_call x1, Pallas kernels, layer(): pl.pallas_call(layer_kernel, out_shape=(jax.ShapeDtypeStruct((TOK, D), BF...  96.4 us
    ppermute x2, waiting for transfers between devices, average(): peer = lax.ppermute(state.astype(BF16), 'rep', pairs)  62.1 us
    ppermute x2, starting transfers between devices, average(): peer = lax.ppermute(state.astype(BF16), 'rep', pairs)  16.9 us
    unnamed x14, local copies, waits for them, and re-layouts  9.68 us
  transfers between devices with their start and end apart: 2, of which 2 were waited for; matrix products, arithmetic and copies ran while one was open for 0% of the time, Pallas kernels for 0%

profile of v1, /device:TPU:40, one launch (start us, length us, event | category | flops | bytes accessed | tf_op | source)
XLA Modules:
  0.0 200.7 jit_solution(5914550845306390412)
XLA Ops:
  0.6 0.0 copy-start.1
  0.6 0.7 broadcast_clamp_fusion
  1.4 0.6 fusion.10
  7.7 1.4 copy.13
  9.1 1.4 copy.12
  10.5 2.3 %copy.14 = bf16[1,1024,352]{2,1,0:T(8,128)(2,1)} copy(bf16[1,1024,352]{1,2,0:T(8,128)(2,1)} %param.25) | data formatting | bytes 1441792 | tf_op args[4]
  12.8 0.0 copy-done.1
  12.8 1.2 copy.15
  14.0 0.0 copy-start.2
  14.0 96.4 %shard_map.113 = (bf16[128,1024]{1,0:T(8,128)(2,1)}, f32[352,1024]{1,0:T(8,128)}) custom-call(bf16[128,1024]{1,0:T(8,128)(2,1)} %bitcast.26, bf16[128,1024]{1,0:T(8,128)(2,1)} %bitcast.27, s32[128,2]{1,0:T(8,128)} %bitcast.23, bf16[128,2]{1,0:T(8,128)(2,1)} %bitcast.24, bf16[1024,352]{1,0:T(8,128)(2,1)} %bitcast.20, bf16[1024,352]{1,0:T(8,128)(2,1)} %bitcast.21, ...), custom_call_target="tpu_custom_call" | custom-call | flops 7000000000 | bytes 6000000 | tf_op jit(solution)/shard_map/pallas_call | solution.py:258
  110.4 0.0 copy-done.2
  110.4 0.1 bitcast_convert_fusion
  110.6 4.9 %conditional.5 = (f32[352,1024]{1,0:T(8,128)S(1)}) conditional(s32[]{:T(128)} %bitcast.10, f32[352,1024]{1,0:T(8,128)S(1)} %bitcast_convert_fusion, f32[352,1024]{1,0:T(8,128)S(1)} %bitcast_convert_fusion, f32[352,1024]{1,0:T(8,128)S(1)} %bitcast_convert_fusion, f32[352,1024]{1,0:T(8,128)S(1)} %bitcast_convert_fusion), branch_computations={%region_0.1_spmd, %region_1.2_spmd, %region_2.3_spmd, %region_3.4_... | conditional | flops 1441792 | bytes 8650800 | solution.py:338
  110.6 0.1 convert_element_type.61
  110.7 1.9 collective-permute-start
  112.6 2.2 %collective-permute-done = bf16[352,1024]{1,0:T(8,128)(2,1)S(1)} collective-permute-done((bf16[352,1024]{1,0:T(8,128)(2,1)S(1)}, bf16[352,1024]{1,0:T(8,128)(2,1)S(1)}, u32[]{:S(2)}, u32[]{:S(2)}) %collective-permute-start) | collective-permute-done | bytes 720928 | tf_op jit(solution)/shard_map/cond/branch_1_fun/ppermute | solution.py:308
  114.8 0.5 add_multiply_fusion
  115.5 3.1 %fusion.8 = (f32[352,1024]{1,0:T(8,128)S(1)}, f32[352,1024]{1,0:T(8,128)}) fusion(f32[352,1024]{1,0:T(8,128)S(1)} %get-tuple-element.109, f32[352,1024]{1,0:T(8,128)} %get-tuple-element.59, bf16[1,352,1024]{2,1,0:T(8,128)(2,1)} %param.29), kind=kLoop, calls=%fused_computation.18 | loop fusion | flops 1441792 | bytes 6488064 | tf_op jit(solution)/shard_map/add | solution.py:340
  118.5 0.0 copy-start
  118.5 1.4 copy-done
  119.9 77.7 %conditional.15 = (f32[352,1024]{1,0:T(8,128)}, f32[352,1024]{1,0:T(8,128)S(1)}, bf16[352,1024]{1,0:T(8,128)(2,1)}) conditional(s32[]{:T(128)} %bitcast.8, (f32[352,1024]{1,0:T(8,128)S(1)}, f32[352,1024]{1,0:T(8,128)S(1)}) %tuple.96, (f32[352,1024]{1,0:T(8,128)S(1)}, f32[352,1024]{1,0:T(8,128)S(1)}) %tuple.97, ...), branch_computations={%region_8.9_spmd, %region_9.10_spmd, %region_10.11_spmd} | conditional | flops 720896 | bytes 10813504
  119.9 1.4 fusion.7
  121.3 14.9 %collective-permute-start.8 = (bf16[352,1024]{1,0:T(8,128)(2,1)S(1)}, bf16[352,1024]{1,0:T(8,128)(2,1)}, u32[]{:S(2)}, u32[]{:S(2)}) collective-permute-start(bf16[352,1024]{1,0:T(8,128)(2,1)S(1)} %get-tuple-element.71), channel_id=1, source_target_pairs={{0,64},{16,80},{32,96},{48,112},{64,0},{80,16},{96,32},{112,48},{1... | collective-permute-start | bytes 2162696 | tf_op jit(solution)/shard_map/cond/branch_2_fun/ppermute | solution.py:308
  136.3 60.0 %collective-permute-done.8 = bf16[352,1024]{1,0:T(8,128)(2,1)} collective-permute-done((bf16[352,1024]{1,0:T(8,128)(2,1)S(1)}, bf16[352,1024]{1,0:T(8,128)(2,1)}, u32[]{:S(2)}, u32[]{:S(2)}) %collective-permute-start.8) | collective-permute-done | bytes 720928 | tf_op jit(solution)/shard_map/cond/branch_2_fun/ppermute | solution.py:308
  196.2 1.4 copy.39
  197.6 0.0 copy-start.3
  197.6 2.4 %fusion.4 = bf16[1,352,1024]{2,1,0:T(8,128)(2,1)} fusion(f32[352,1024]{1,0:T(8,128)S(1)} %copy-done, f32[352,1024]{1,0:T(8,128)S(1)} %get-tuple-element.60, bf16[352,1024]{1,0:T(8,128)(2,1)} %get-tuple-element.66), kind=kLoop, calls=%fused_computation.12 | loop fusion | flops 1802240 | bytes 4325376 | tf_op jit(solution)/shard_map/broadcast_in_dim | solution.py:342
  200.0 0.0 copy-done.3
  200.0 0.7 copy.40
  (1 shorter events, 0.0 us)
Async XLA Ops:
  0.6 12.2 %copy-start.1 = (bf16[1,1024,352]{1,2,0:T(8,128)(2,1)S(1)}, bf16[1,1024,352]{1,2,0:T(8,128)(2,1)}, u32[]{:S(2)}) copy-start(bf16[1,1024,352]{1,2,0:T(8,128)(2,1)} %param.26) | copy-start | bytes 2162692
  14.0 96.4 %copy-start.2 = (bf16[1,352,1024]{2,1,0:T(8,128)(2,1)S(1)}, bf16[1,352,1024]{2,1,0:T(8,128)(2,1)}, u32[]{:S(2)}) copy-start(bf16[1,352,1024]{2,1,0:T(8,128)(2,1)} %param.28) | copy-start | bytes 2162692
  110.7 4.1 %collective-permute-start = (bf16[352,1024]{1,0:T(8,128)(2,1)S(1)}, bf16[352,1024]{1,0:T(8,128)(2,1)S(1)}, u32[]{:S(2)}, u32[]{:S(2)}) collective-permute-start(bf16[352,1024]{1,0:T(8,128)(2,1)S(1)} %convert_element_type.61), channel_id=1, source_target_pairs={{0,16},{16,0},{32,48},{48,32},{64,80},{80,64},{96,112},{112,96},{1... | collective-permute-start | bytes 2162696 | tf_op jit(solution)/shard_map/cond/branch_1_fun/ppermute | solution.py:308
  118.5 1.4 copy-start
  121.3 74.9 %collective-permute-start.8 = (bf16[352,1024]{1,0:T(8,128)(2,1)S(1)}, bf16[352,1024]{1,0:T(8,128)(2,1)}, u32[]{:S(2)}, u32[]{:S(2)}) collective-permute-start(bf16[352,1024]{1,0:T(8,128)(2,1)S(1)} %get-tuple-element.71), channel_id=1, source_target_pairs={{0,64},{16,80},{32,96},{48,112},{64,0},{80,16},{96,32},{112,48},{1... | collective-permute-start | bytes 2162696 | tf_op jit(solution)/shard_map/cond/branch_2_fun/ppermute | solution.py:308
  197.6 2.4 %copy-start.3 = (bf16[128,1024]{1,0:T(8,128)(2,1)S(1)}, bf16[128,1024]{1,0:T(8,128)(2,1)}, u32[]{:S(2)}) copy-start(bf16[128,1024]{1,0:T(8,128)(2,1)} %get-tuple-element.58) | copy-start | bytes 786436
